TPU v7x, 32 devices: a whole 2x2x4 slice. The times are simulated.
32 devices in a mesh: grp: 2 (over y), dp: 8 (over z, x), mp: 2 (over core).
Axes of the slice: x: 2, y: 2, z: 4, core: 2. Of those that a mesh axis runs over, the one named last changes fastest.
Arguments:
- cand_x: bfloat16 [384, 16, 5120], P(('grp', 'dp')), parts along dimension 0
- val_x: bfloat16 [256, 16, 5120], P(('grp', 'dp')), parts along dimension 0
- cand_grad: bfloat16 [384, 16, 5120], P(('grp', 'dp')), parts along dimension 0
- val_grad: bfloat16 [256, 16, 5120], P(('grp', 'dp')), parts along dimension 0
- cand_attn: bfloat16 [384, 16, 5120], P(('grp', 'dp'), None, 'mp'), parts along dimension 0
- val_attn: bfloat16 [256, 16, 5120], P(('grp', 'dp'), None, 'mp'), parts along dimension 0
- cand_probs: bfloat16 [384, 40, 16, 16], P(('grp', 'dp'), 'mp'), parts along dimension 0, as said below
- val_probs: bfloat16 [256, 40, 16, 16], P(('grp', 'dp'), 'mp'), parts along dimension 0, as said below
- cand_len: int32 [384], P(('grp', 'dp')), parts along dimension 0, may hold values from 4 to 16, as said below
- val_len: int32 [256], P(('grp', 'dp')), parts along dimension 0, may hold values from 4 to 16, as said below
- out_weight: bfloat16 [5120, 5120], P('mp', 'dp'), may hold values from -0.078125 to 0.078125
- input_proj: bfloat16 [5120, 64], replicated, may hold values from -0.078125 to 0.078125
- grad_proj: bfloat16 [5120, 128], replicated, may hold values from -0.078125 to 0.078125
- attn_proj: bfloat16 [5120, 64], P('mp'), may hold values from -0.078125 to 0.078125
- value_proj: bfloat16 [1024, 128], P('mp'), may hold values from -0.1875 to 0.1875
Outputs:
- scores: float32 [384, 128], P(('grp', 'dp')), parts along dimension 0
There are 2 independent parts, one for each index of `grp`. A program takes and returns all parts, laid end to end along the dimension named above; an argument that names none is the same for every part. Nothing has to cross between parts.
Inputs may be any that keep to these rules, and one draw needn't show every extreme that they name: `cand_len`: each prompt has at least 4 live tokens; some prompt of each set is full. `val_len`: each prompt has at least 4 live tokens; some prompt of each set is full. `cand_probs`: Causal: entries with key after query are zero; each query row sums to one up to rounding. `val_probs`: Causal: entries with key after query are zero; each query row sums to one up to rounding.
All inputs are finite; a program needn't handle non-finite values.
Results may differ from a plain program's by a relative error of at most 0.0022.
Values may be sent and summed in bfloat16 or wider, within the bound.
A program may use at most 192 MiB of HBM per device.

v0:
```python
import jax
import jax.numpy as jnp
from jax import lax
from jax.sharding import PartitionSpec as P

HEAD_DIM = 128


def outer_sum(left, right):
    count = left.shape[0]
    return jnp.einsum("eta,etb->eab", left, right).reshape(count, left.shape[2] * right.shape[2])


def normalized(feat):
    totals = jnp.sum(feat * feat, axis=1, keepdims=True)
    return (feat * lax.rsqrt(totals + 1e-06)).astype(jnp.bfloat16)


def local(
    cand_x,
    val_x,
    cand_grad,
    val_grad,
    cand_attn,
    val_attn,
    cand_probs,
    val_probs,
    cand_len,
    val_len,
    out_weight,
    input_proj,
    grad_proj,
    attn_proj,
    value_proj,
):
    n_cand = cand_x.shape[0]
    inputs = jnp.concatenate([cand_x, val_x], axis=0)
    grads = jnp.concatenate([cand_grad, val_grad], axis=0)
    attn = jnp.concatenate([cand_attn, val_attn], axis=0)
    probs = jnp.concatenate([cand_probs, val_probs], axis=0)
    length = jnp.concatenate([cand_len, val_len], axis=0)
    count, seq, width = inputs.shape
    tokens = count * seq
    positions = jnp.arange(seq, dtype=jnp.int32)
    mask = (positions[None, :] < length[:, None]).astype(jnp.bfloat16)
    flat_grad = (grads * mask[:, :, None]).reshape(tokens, width)
    grad_attn = lax.dot_general(
        flat_grad,
        lax.all_gather(out_weight, "dp", axis=1, tiled=True),
        (((1,), (1,)), ((), ())),
        preferred_element_type=jnp.float32,
    ).astype(jnp.bfloat16)
    local_heads = probs.shape[1]
    grad_heads = grad_attn.reshape(count, seq, local_heads, HEAD_DIM)
    mixed = jnp.einsum("ehij,eihd->ejhd", probs, grad_heads, preferred_element_type=jnp.float32)
    local_kv = value_proj.shape[0] // HEAD_DIM
    group = local_heads // local_kv
    grad_value = jnp.sum(mixed.reshape(count, seq, local_kv, group, HEAD_DIM), axis=3)
    grad_value = grad_value.reshape(tokens, local_kv * HEAD_DIM).astype(jnp.bfloat16)
    a_in = jnp.dot(
        inputs.reshape(tokens, width), input_proj, preferred_element_type=jnp.float32
    ).reshape(count, seq, -1)
    b_val = jnp.dot(grad_value, value_proj, preferred_element_type=jnp.float32).reshape(
        count, seq, -1
    )
    a_att = jnp.dot(
        attn.reshape(tokens, attn.shape[2]), attn_proj, preferred_element_type=jnp.float32
    ).reshape(count, seq, -1)
    b_out = jnp.dot(flat_grad, grad_proj, preferred_element_type=jnp.float32).reshape(
        count, seq, -1
    )
    partial_value = jnp.concatenate([outer_sum(a_att, b_out), outer_sum(a_in, b_val)], axis=1)
    unit = normalized(lax.psum(partial_value, "mp"))
    return lax.dot_general(
        unit[:n_cand],
        lax.all_gather(unit[n_cand:], "dp", axis=0, tiled=True),
        (((1,), (1,)), ((), ())),
        preferred_element_type=jnp.float32,
    )


def solution(mesh):
    placed = (
        P(("grp", "dp"), None, None),
        P(("grp", "dp"), None, None),
        P(("grp", "dp"), None, None),
        P(("grp", "dp"), None, None),
        P(("grp", "dp"), None, "mp"),
        P(("grp", "dp"), None, "mp"),
        P(("grp", "dp"), "mp", None, None),
        P(("grp", "dp"), "mp", None, None),
        P(("grp", "dp")),
        P(("grp", "dp")),
        P("mp", "dp"),
        P(),
        P(),
        P("mp", None),
        P("mp", None),
    )
    return jax.shard_map(
        local, mesh=mesh, in_specs=placed, out_specs=P(("grp", "dp"), None), check_vma=False
    )
```

profile of v0, /device:TPU:0, one launch (start us, length us, event | category | flops | bytes accessed | tf_op | source)
XLA Modules:
  0.0 674.9 jit_solution(10452645793433025643)
XLA Ops:
  6.5 0.0 copy-start
  6.5 0.0 copy-start.10
  6.5 0.0 all-gather.3.cloned.1.call-start
  6.5 0.7 all-gather.3.cloned.1.call-update
  7.3 0.0 all-reduce.2.cloned.1.call-start
  7.3 0.0 copy-done.10
  7.3 0.0 copy-done.9
  7.3 0.1 pad_add_fusion
  7.4 0.1 fusion.37
  7.5 0.1 reshape.73
  7.6 3.9 copy.29
  11.4 4.0 copy.30
  15.5 0.0 copy-start.5
  15.5 2.5 constant_dynamic-update-slice_fusion.1
  18.0 0.6 copy-done.5
  18.6 0.2 constant_dynamic-update-slice_fusion
  18.8 0.0 copy-start.2
  18.8 2.7 copy-done.2
  21.5 0.0 copy-done
  21.5 1.9 fusion.4
  23.4 4.6 fusion.21
  28.0 6.1 bitcast_multiply_fusion
  34.2 477.6 %all-gather.3.cloned.1.call-done = bf16[2560,5120]{1,0:T(8,128)(2,1)} async-done(((bf16[2560,640]{1,0:T(8,128)(2,1)}), bf16[2560,5120]{1,0:T(8,128)(2,1)}) %all-gather.3.cloned.1.call-update) | async-done | bytes 26214416 | tf_op jit(solution)/shard_map/all_gather | solution.py:49
  511.7 23.3 %convolution_convert_fusion = bf16[640,2560]{1,0:T(8,128)(2,1)} fusion(bf16[640,5120]{1,0:T(8,128)(2,1)} %bitcast_multiply_fusion, bf16[2560,5120]{1,0:T(8,128)(2,1)} %all-gather.3.cloned.1.call-done), kind=kOutput, calls=%fused_computation.7 | convolution fusion | flops 16778854400 | bytes 36044800 | tf_op jit(solution)/shard_map/dot_general | solution.py:47
  535.0 0.0 copy-start.4
  535.0 6.9 %reshape.70 = bf16[40,16,20,128]{3,2,1,0:T(8,128)(2,1)} reshape(bf16[640,2560]{1,0:T(8,128)(2,1)} %convolution_convert_fusion) | data formatting | bytes 6553600 | tf_op jit(solution)/shard_map/reshape | solution.py:54
  541.9 0.0 copy-done.4
  541.9 6.7 fusion.10
  548.6 0.0 copy-start.7
  548.6 3.8 reduce_sum.18
  552.4 0.0 copy-done.7
  552.4 0.0 copy-done.8
  552.4 0.0 copy-start.6
  552.5 6.7 fusion.18
  559.1 0.0 copy-done.6
  559.1 3.0 copy_bitcast_fusion
  562.1 1.7 pad_maximum_fusion
  563.8 0.0 all-reduce.2.cloned.1.call-update
  563.8 0.0 all-gather.5.cloned.1.call-start
  563.8 22.3 %all-reduce.2.cloned.1.call-done = f32[40,16384]{1,0:T(8,128)} async-done(((f32[40,16384]{1,0:T(8,128)}), f32[40,16384]{1,0:T(8,128)}) %all-reduce.2.cloned.1.call-update) | async-done | bytes 2621456 | tf_op jit(solution)/shard_map/psum | solution.py:73
  586.1 2.2 multiply_reduce_fusion
  588.3 0.4 copy-done.3
  588.6 0.2 multiply_convert_fusion
  588.8 0.8 slice.9
  589.7 0.0 all-gather.5.cloned.1.call-update
  589.7 74.7 %all-gather.5.cloned.1.call-done = bf16[128,16384]{1,0:T(8,128)(2,1)} async-done(((bf16[16,16384]{1,0:T(8,128)(2,1)}), bf16[128,16384]{1,0:T(8,128)(2,1)}) %all-gather.5.cloned.1.call-update) | async-done | bytes 4194320 | tf_op jit(solution)/shard_map/all_gather | solution.py:76
  664.4 4.0 fusion.25
  668.4 0.0 copy-done.1
  (5 shorter events, 0.0 us)
Async XLA Ops:
  6.5 15.0 %copy-start = (bf16[5120,128]{1,0:T(8,128)(2,1)S(1)}, bf16[5120,128]{1,0:T(8,128)(2,1)}, u32[]{:S(2)}) copy-start(bf16[5120,128]{1,0:T(8,128)(2,1)} %param.27) | copy-start | bytes 3932164
  6.5 0.8 copy-start.10
  6.5 0.8 copy-start.9
  6.5 505.2 %all-gather.3.cloned.1.call-start = ((), (), s32[]{:S(2)}) async-start(), calls=%async_computation | async-start | bytes 29491200 | tf_op jit(solution)/shard_map/all_gather | solution.py:49
  7.3 578.8 %all-reduce.2.cloned.1.call-start = ((), (), s32[]{:S(2)}) async-start(), calls=%async_computation.1 | async-start | bytes 5242880 | tf_op jit(solution)/shard_map/psum | solution.py:73
  15.5 3.1 copy-start.5
  18.8 2.7 copy-start.2
  535.0 6.9 %copy-start.4 = (bf16[16,20,16,16]{2,3,1,0:T(8,128)(2,1)S(1)}, bf16[16,20,16,16]{2,3,1,0:T(8,128)(2,1)}, u32[]{:S(2)}) copy-start(bf16[16,20,16,16]{2,3,1,0:T(8,128)(2,1)} %copy.30) | copy-start | bytes 491524
  548.6 3.8 copy-start.7
  548.6 3.8 copy-start.8
  552.4 6.7 copy-start.6
  563.8 100.6 %all-gather.5.cloned.1.call-start = ((), (), s32[]{:S(2)}) async-start(), calls=%async_computation.2 | async-start | bytes 4718592 | tf_op jit(solution)/shard_map/all_gather | solution.py:76
  586.1 2.5 copy-start.3
  588.6 79.8 %copy-start.1 = (bf16[5120,128]{1,0:T(8,128)(2,1)S(1)}, bf16[5120,128]{1,0:T(8,128)(2,1)}, u32[]{:S(2)}) copy-start(bf16[5120,128]{1,0:T(8,128)(2,1)} %param.27) | copy-start | bytes 3932164
Sparse Core Ops, SparseCore 0:
  8.9 502.7 all-gather.2
  563.9 22.1 all-reduce.1
  589.8 74.5 all-gather.4
where the time goes:
time: 675 us
  waiting for transfers between devices  575 us (85%)
  matrix products  47.1 us (7%)
  local copies, waits for them, and re-layouts  25.1 us (4%)
  other arithmetic  14.2 us (2%)
  between operations  13.2 us (2%)
    all_gather x1, waiting for transfers between devices, local(): lax.all_gather(out_weight, 'dp', axis=1, tiled=True)  478 us
    all_gather x1, waiting for transfers between devices, local(): lax.all_gather(unit[n_cand:], 'dp', axis=0, tiled=True)  74.7 us
    dot_general x1, matrix products, local(): lax.dot_general(flat_grad, lax.all_gather(out_weight, 'dp', axis=1, tiled...  23.3 us
    psum x1, waiting for transfers between devices, local(): unit = normalized(lax.psum(partial_value, 'mp'))  22.3 us
    unnamed x25, local copies, waits for them, and re-layouts  14.1 us
  transfers between devices with their start and end apart: 3, of which 3 were waited for; matrix products, arithmetic and copies ran while one was open for 3% of the time, Pallas kernels for 0%

commit v1 on v0

v1 whole, which is shorter than its diff:
```python
import jax
import jax.numpy as jnp
from jax import lax
from jax.sharding import PartitionSpec as P

HEAD_DIM = 128
EPS = 1e-06


def dot(left, right, contract):
    return lax.dot_general(
        left, right, ((contract[:1], contract[1:]), ((), ())), preferred_element_type=jnp.float32
    )


def gram(left_a, left_b, right_a, right_b):
    return dot(left_a, right_a, (1, 1)) * dot(left_b, right_b, (1, 1))


def own(cand, val, n_mp, index):
    cand_rows, val_rows = cand.shape[0] // n_mp, val.shape[0] // n_mp
    return jnp.concatenate(
        [
            lax.dynamic_slice_in_dim(cand, index * cand_rows, cand_rows, 0),
            lax.dynamic_slice_in_dim(val, index * val_rows, val_rows, 0),
        ],
        axis=0,
    )


def regroup(cand, val, n_mp):
    cand = cand.reshape((n_mp, cand.shape[0] // n_mp) + cand.shape[1:])
    val = val.reshape((n_mp, val.shape[0] // n_mp) + val.shape[1:])
    both = jnp.concatenate([cand, val], axis=1)
    return both.reshape((both.shape[0] * both.shape[1],) + both.shape[2:])


def folded(out_weight, value_proj, local_heads):
    local_kv = value_proj.shape[0] // HEAD_DIM
    group = local_heads // local_kv
    weight = out_weight.reshape(local_kv, group, HEAD_DIM, out_weight.shape[1])
    proj = value_proj.reshape(local_kv, HEAD_DIM, value_proj.shape[1])
    fold = jnp.einsum("kgdf,kdb->fkgb", weight, proj, preferred_element_type=jnp.float32)
    return fold.reshape(out_weight.shape[1], local_heads, -1).astype(jnp.bfloat16)


def local(n_mp, cand_x, val_x, cand_grad, val_grad, cand_attn, val_attn, cand_probs, val_probs,
          cand_len, val_len, out_weight, input_proj, grad_proj, attn_proj, value_proj):
    index = lax.axis_index("mp")
    seq, width = cand_x.shape[1:]
    n_cand = cand_x.shape[0] // n_mp
    count = n_cand + val_x.shape[0] // n_mp
    tokens = count * seq
    heads = cand_probs.shape[1]
    features = out_weight.shape[1]
    n_dp = width // features
    positions = jnp.arange(seq, dtype=jnp.int32)

    grads = own(cand_grad, val_grad, n_mp, index).reshape(tokens, width)
    inputs = own(cand_x, val_x, n_mp, index).reshape(tokens, width)
    length = regroup(cand_len, val_len, n_mp)
    probs = regroup(cand_probs, val_probs, n_mp)
    mask = positions[None, :] < length[:, None]
    probs = jnp.where(mask[:, None, :, None], probs, 0)
    probs = probs.transpose(0, 3, 1, 2).reshape(n_mp * tokens, heads, seq)
    probs = lax.all_to_all(probs, "mp", 0, 1, tiled=True)
    attn = regroup(cand_attn, val_attn, n_mp).reshape(n_mp * tokens, -1)

    spread = lax.all_to_all(grads.reshape(tokens, n_dp, features), "dp", 1, 0, tiled=True)
    spread = spread.reshape(n_dp * count * seq, features)
    probs = lax.all_gather(probs, "dp", axis=0, tiled=True)
    fold = lax.all_gather(folded(out_weight, value_proj, heads), "mp", axis=1, tiled=True)
    all_heads = heads * n_mp
    mixed = dot(spread, fold.reshape(features, -1), (1, 0)).astype(jnp.bfloat16)
    mixed = mixed.reshape(n_dp * count, seq, all_heads, -1)
    probs = probs.reshape(n_dp * count, seq, all_heads, seq)
    b_val = jnp.einsum("ejhi,eihb->ejb", probs, mixed, preferred_element_type=jnp.float32)
    b_val = lax.psum_scatter(b_val, "dp", scatter_dimension=0, tiled=True).reshape(tokens, -1)

    a_in = dot(inputs, input_proj, (1, 0)).astype(jnp.bfloat16)
    live = (positions[None, :] < own(cand_len, val_len, n_mp, index)[:, None]).reshape(tokens, 1)
    b_out = jnp.where(live, dot(grads, grad_proj, (1, 0)), 0.0)
    a_att = dot(attn, attn_proj, (1, 0))
    a_att = lax.psum_scatter(a_att, "mp", scatter_dimension=0, tiled=True).astype(jnp.bfloat16)

    low_out, low_val = b_out.astype(jnp.bfloat16), b_val.astype(jnp.bfloat16)
    square = gram(a_att, low_out, a_att, low_out) + gram(a_in, low_val, a_in, low_val)
    which = jnp.arange(tokens) // seq
    total = jnp.sum(jnp.where(which[:, None] == which[None, :], square, 0.0), axis=1)
    total = jnp.sum(total.reshape(count, seq), axis=1)
    scale = jnp.repeat(lax.rsqrt(jnp.maximum(total, 0.0) + EPS), seq)[:, None]
    factors = jnp.concatenate(
        [a_att, a_in, (b_out * scale).astype(jnp.bfloat16), (b_val * scale).astype(jnp.bfloat16)], axis=1
    )
    rows = n_cand * seq
    ours = factors[:rows]
    theirs = lax.all_gather(factors[rows:], ("dp", "mp"), axis=0, tiled=True)
    ka, kb = a_in.shape[1], b_out.shape[1]
    cuts = (slice(0, ka), slice(2 * ka, 2 * ka + kb), slice(ka, 2 * ka), slice(2 * ka + kb, None))
    first, second, third, fourth = [(ours[:, cut], theirs[:, cut]) for cut in cuts]
    product = gram(first[0], second[0], first[1], second[1]) + gram(third[0], fourth[0], third[1], fourth[1])
    scores = jnp.sum(product.reshape(n_cand, seq, -1, seq), axis=(1, 3))
    return lax.all_gather(scores, "mp", axis=0, tiled=True)


def solution(mesh):
    placed = (
        P(("grp", "dp"), None, None),
        P(("grp", "dp"), None, None),
        P(("grp", "dp"), None, None),
        P(("grp", "dp"), None, None),
        P(("grp", "dp"), None, "mp"),
        P(("grp", "dp"), None, "mp"),
        P(("grp", "dp"), "mp", None, None),
        P(("grp", "dp"), "mp", None, None),
        P(("grp", "dp")),
        P(("grp", "dp")),
        P("mp", "dp"),
        P(),
        P(),
        P("mp", None),
        P("mp", None),
    )

    def body(*args):
        return local(mesh.shape["mp"], *args)

    return jax.shard_map(
        body, mesh=mesh, in_specs=placed, out_specs=P(("grp", "dp"), None), check_vma=False
    )
```

time: 675 us -> 432 us (0.64)
  waiting for transfers between devices: 575 us -> 231 us
  local copies, waits for them, and re-layouts: 25.1 us -> 91.1 us
  matrix products: 47.1 us -> 60.6 us
  starting transfers between devices: 0.08 us -> 7.77 us
    all_gather x2 -> x3, waiting for transfers between devices: 552 us -> 51.9 us  [the longest x1 38.8 us: local(): theirs = lax.all_gather(factors[rows:], ('dp', 'mp'), axis=0, tiled=True)]
    all_to_all x0 -> x1, waiting for transfers between devices: none -> 125 us  [local(): lax.all_to_all(grads.reshape(tokens, n_dp, features), 'dp', 1, 0, tiled=T...]
    reduce_scatter x0 -> x2, waiting for transfers between devices: none -> 53.9 us  [the longest x1 53.8 us: local(): lax.psum_scatter(b_val, 'dp', scatter_dimension=0, tiled=True)]
    unnamed x25 -> x30, local copies, waits for them, and re-layouts: 14.1 us -> 39.5 us
    psum x1 -> x0, waiting for transfers between devices: 22.3 us -> none  [local(): unit = normalized(lax.psum(partial_value, 'mp'))]
    reshape x2 -> x6, local copies, waits for them, and re-layouts: 9.83 us -> 23.2 us  [the longest x1 8.43 us: local(): scores = jnp.sum(product.reshape(n_cand, seq, -1, seq), axis=(1, 3))]
    dot_general x6 -> x13, matrix products: 47.1 us -> 58.8 us  [the longest x11 39.7 us: dot(): lax.dot_general(left, right, ((contract[:1], contract[1:]), ((), ())), pr...]
    all_gather x0 -> x1, local copies, waits for them, and re-layouts: none -> 9.55 us  [local(): lax.all_gather(folded(out_weight, value_proj, heads), 'mp', axis=1, tiled...]
  transfers between devices with their start and end apart: 3 -> 6, of which waited for: 3 -> 4; matrix products, arithmetic and copies ran while one was open for 3% -> 31% of each run, Pallas kernels for 0% -> 0%
where the time goes in v1:
time: 432 us; the launch traced here: 430 us
  waiting for transfers between devices  231 us (53%)
  local copies, waits for them, and re-layouts  91.1 us (21%)
  matrix products  60.6 us (14%)
  other arithmetic  19.7 us (5%)
  between operations  13.4 us (3%)
  starting transfers between devices  7.77 us (2%)
  blocking collectives  6.73 us (2%)
    all_to_all x1, waiting for transfers between devices, local(): lax.all_to_all(grads.reshape(tokens, n_dp, features), 'dp', 1, 0, tiled=T...  125 us
    reduce_scatter x1, waiting for transfers between devices, local(): lax.psum_scatter(b_val, 'dp', scatter_dimension=0, tiled=True)  53.8 us
    dot_general x11, matrix products, dot(): lax.dot_general(left, right, ((contract[:1], contract[1:]), ((), ())), pr...  39.7 us
    unnamed x30, local copies, waits for them, and re-layouts  39.5 us
    all_gather x1, waiting for transfers between devices, local(): theirs = lax.all_gather(factors[rows:], ('dp', 'mp'), axis=0, tiled=True)  38.8 us
    dot_general x1, matrix products, local(): jnp.einsum('ejhi,eihb->ejb', probs, mixed, preferred_element_type=jnp.flo...  15.4 us
    all_gather x1, waiting for transfers between devices, local(): probs = lax.all_gather(probs, 'dp', axis=0, tiled=True)  13.1 us
    all_gather x1, local copies, waits for them, and re-layouts, local(): lax.all_gather(folded(out_weight, value_proj, heads), 'mp', axis=1, tiled...  9.55 us
  transfers between devices with their start and end apart: 6, of which 4 were waited for; matrix products, arithmetic and copies ran while one was open for 31% of the time, Pallas kernels for 0%

profile of v1, /device:TPU:0, one launch (start us, length us, event | category | flops | bytes accessed | tf_op | source)
XLA Modules:
  0.0 430.4 jit_solution(15865198508572348106)
XLA Ops:
  6.5 1.9 copy-done
  8.5 3.6 convolution_convert_fusion.1
  12.1 5.6 %copy.69 = bf16[640,20,128]{2,0,1:T(8,128)(2,1)} copy(bf16[640,20,128]{0,2,1:T(8,128)(2,1)} %bitcast.75) | data formatting | bytes 6553600 | tf_op jit(solution)/shard_map/convert_element_type | solution.py:44
  17.7 1.2 copy-done.3
  19.0 3.3 copy.61
  22.3 3.2 pad_maximum_fusion.3
  25.5 7.8 %copy.62 = bf16[40,20,16,16]{3,0,2,1:T(8,128)(2,1)S(1)} copy(bf16[40,20,16,16]{1,3,2,0:T(8,128)(2,1)} %bitcast.79) | data formatting | bytes 819200 | tf_op jit(solution)/shard_map/reshape | solution.py:35
  33.7 2.2 select_bitcast_fusion
  35.9 6.7 %copy.75 = bf16[40,16,20,16]{2,3,1,0:T(8,128)(2,1)S(1)} copy(bf16[40,16,20,16]{1,0,3,2:T(8,128)(2,1)} %select_bitcast_fusion) | data formatting | bytes 819200 | tf_op jit(solution)/shard_map/reshape | solution.py:65
  42.6 5.7 %reshape.153 = bf16[2,2,51200]{2,1,0:T(2,128)(2,1)S(1)} reshape(bf16[640,16,20]{2,1,0:T(8,128)(2,1)S(1)} %bitcast.80) | data formatting | bytes 819200
  48.4 4.9 %all_to_all.33 = bf16[2,2,51200]{2,1,0:T(2,128)(2,1)} all-to-all(bf16[2,2,51200]{2,1,0:T(2,128)(2,1)S(1)} %reshape.153), channel_id=1, replica_groups=mesh['grp'=2,'dp'=8,'mp'=2] {'mp'}, dimensions={0} | all-to-all | bytes 819200 | tf_op jit(solution)/shard_map/all_to_all | solution.py:66
  53.3 7.7 %reshape.154 = bf16[640,16,20]{2,1,0:T(8,128)(2,1)S(1)} reshape(bf16[2,2,51200]{2,1,0:T(2,128)(2,1)} %all_to_all.33) | data formatting | bytes 819200
  61.0 2.9 copy.76
  64.0 1.8 copy.66
  65.9 3.9 constant_dynamic-slice_fusion.1
  70.0 1.2 constant_dynamic-slice_fusion
  71.5 0.6 copy.81
  72.1 2.1 copy.67
  74.2 7.1 %all-to-all-start.1 = ((bf16[320,8,640]{2,0,1:T(8,128)(2,1)}), bf16[320,8,640]{2,0,1:T(8,128)(2,1)}, u32[]{:S(2)}, u32[]{:S(2)}) async-start(bf16[320,8,640]{2,0,1:T(8,128)(2,1)} %copy.67), calls=%async_computation.1 | async-start | bytes 6553600 | tf_op jit(solution)/shard_map/all_to_all | solution.py:69
  81.4 2.3 pad_maximum_fusion
  83.7 1.7 fusion.28
  85.7 9.5 %copy.70 = bf16[640,40,128]{0,2,1:T(8,128)(2,1)} copy(bf16[640,40,128]{2,0,1:T(8,128)(2,1)} %all-gather.7.cloned.1.call-done) | data formatting | bytes 13107200 | tf_op jit(solution)/shard_map/all_gather | solution.py:72
  95.3 125.3 %all-to-all-done.1 = bf16[320,8,640]{2,0,1:T(8,128)(2,1)} async-done(((bf16[320,8,640]{2,0,1:T(8,128)(2,1)}), bf16[320,8,640]{2,0,1:T(8,128)(2,1)}, u32[]{:S(2)}, u32[]{:S(2)}) %all-to-all-start.1) | async-done | bytes 3276832 | tf_op jit(solution)/shard_map/all_to_all | solution.py:69
  220.6 27.6 %fusion.2 = bf16[320,8,40,128]{3,1,2,0:T(8,128)(2,1)} fusion(bf16[2560,640]{1,0:T(8,128)(2,1)} %bitcast.16, bf16[640,5120]{0,1:T(8,128)(2,1)} %bitcast.82), kind=kOutput, calls=%fused_computation.3 | convolution fusion | flops 16790323200 | bytes 36044800 | tf_op jit(solution)/shard_map/dot_general | solution.py:11
  248.3 18.1 %copy.82 = bf16[320,8,40,128]{3,2,1,0:T(8,128)(2,1)} copy(bf16[320,8,40,128]{3,1,2,0:T(8,128)(2,1)} %fusion.2) | data formatting | bytes 52428800
  266.4 13.1 %all-gather.5.cloned.1.call-done = bf16[2560,40,16]{1,2,0:T(8,128)(2,1)} async-done(((bf16[320,40,16]{1,2,0:T(8,128)(2,1)}), bf16[2560,40,16]{1,2,0:T(8,128)(2,1)}) %all-gather.5.cloned.1.call-update) | async-done | bytes 3276816 | tf_op jit(solution)/shard_map/all_gather | solution.py:71
  279.4 15.4 %fusion.5 = f32[160,16,128]{2,1,0:T(8,128)} fusion(bf16[160,16,40,16]{2,3,1,0:T(8,128)(2,1)} %bitcast.76, bf16[160,16,40,128]{3,2,1,0:T(8,128)(2,1)} %bitcast.72), kind=kOutput, calls=%fused_computation.14 | convolution fusion | flops 419430400 | bytes 30801920 | tf_op jit(solution)/shard_map/ejhi,eihb->ejb/dot_general | solution.py:77
  294.9 0.3 all-gather.9.cloned.1.call-start
  295.6 2.3 pad_maximum_fusion.1
  297.9 1.1 convolution_convert_fusion.2
  299.0 0.7 copy.72
  299.8 1.1 fusion.30
  300.8 2.3 convolution_select_fusion
  303.2 0.9 convert_element_type.36
  304.4 53.8 %reduce-scatter.5.cloned.1.call-done = f32[20,16,128]{2,1,0:T(8,128)} async-done(((f32[160,16,128]{2,1,0:T(8,128)}), f32[20,16,128]{2,1,0:T(8,128)}) %reduce-scatter.5.cloned.1.call-update) | async-done | bytes 163856 | tf_op jit(solution)/shard_map/reduce_scatter | solution.py:78
  358.2 0.9 convert_element_type.43
  359.1 1.3 convolution_multiply_fusion.2
  361.0 1.0 multiply_convert_fusion
  362.1 0.7 pad_maximum_fusion.4
  362.9 38.8 %all-gather.9.cloned.1.call-done = bf16[2048,384]{1,0:T(8,128)(2,1)} async-done(((bf16[128,384]{1,0:T(8,128)(2,1)}), bf16[2048,384]{1,0:T(8,128)(2,1)}) %all-gather.9.cloned.1.call-update) | async-done | bytes 1572880 | tf_op jit(solution)/shard_map/all_gather | solution.py:97
  401.7 1.5 fusion.17
  403.2 1.6 fusion.14
  404.8 1.2 convolution_multiply_fusion
  405.9 1.6 fusion.4
  407.6 8.4 %reshape.146 = f32[12,16,128,16]{3,2,1,0:T(8,128)} reshape(f32[192,2048]{1,0:T(8,128)} %fusion.4) | data formatting | bytes 3145728 | tf_op jit(solution)/shard_map/reshape | solution.py:102
  416.0 5.5 %reduce_sum.29 = f32[12,128]{1,0:T(8,128)S(1)} reduce(f32[12,16,128,16]{3,2,1,0:T(8,128)} %reshape.146, f32[]{:T(128)} %constant.32.clone.1), dimensions={1,3}, to_apply=%region_4.5 | reduce | flops 391680 | bytes 1579012 | tf_op jit(solution)/shard_map/reduce_sum | solution.py:102
  421.5 1.8 all-gather
  423.3 0.6 reshape.148
  (53 shorter events, 2.6 us)
Async XLA Ops:
  6.5 1.9 copy-start
  6.5 79.2 %all-gather.7.cloned.1.call-start = ((), (), s32[]{:S(2)}) async-start(), calls=%async_computation.5 | async-start | bytes 9830400 | tf_op jit(solution)/shard_map/all_gather | solution.py:72
  17.7 1.3 copy-start.3
  17.7 261.7 %all-gather.5.cloned.1.call-start = ((), (), s32[]{:S(2)}) async-start(), calls=%async_computation.4 | async-start | bytes 11796480 | tf_op jit(solution)/shard_map/all_gather | solution.py:71
  25.5 7.8 %copy-start.10 = (s32[24]{0:T(128)S(1)}, s32[24]{0:T(128)}, u32[]{:S(2)}) copy-start(s32[24]{0:T(128)} %param.23) | copy-start | bytes 292
  25.5 7.9 %copy-start.11 = (s32[16]{0:T(128)S(1)}, s32[16]{0:T(128)}, u32[]{:S(2)}) copy-start(s32[16]{0:T(128)} %param.24) | copy-start | bytes 196
  65.9 3.9 copy-start.5
  65.9 4.1 copy-start.6
  74.2 146.4 %all-to-all-start.1 = ((bf16[320,8,640]{2,0,1:T(8,128)(2,1)}), bf16[320,8,640]{2,0,1:T(8,128)(2,1)}, u32[]{:S(2)}, u32[]{:S(2)}) async-start(bf16[320,8,640]{2,0,1:T(8,128)(2,1)} %copy.67), calls=%async_computation.1 | async-start | bytes 6553600 | tf_op jit(solution)/shard_map/all_to_all | solution.py:69
  81.3 221.9 %reduce-scatter.7.cloned.1.call-start = ((), (), s32[]{:S(2)}) async-start(), calls=%async_computation.8 | async-start | bytes 491520 | tf_op jit(solution)/shard_map/reduce_scatter | solution.py:84
  81.4 2.3 copy-start.9
  85.4 272.8 %reduce-scatter.5.cloned.1.call-start = ((), (), s32[]{:S(2)}) async-start(), calls=%async_computation.6 | async-start | bytes 1474560 | tf_op jit(solution)/shard_map/reduce_scatter | solution.py:78
  294.9 106.8 %all-gather.9.cloned.1.call-start = ((), (), s32[]{:S(2)}) async-start(), calls=%async_computation.7 | async-start | bytes 1671168 | tf_op jit(solution)/shard_map/all_gather | solution.py:97
  295.6 2.3 copy-start.4
  303.2 58.9 %copy-start.8 = (bf16[320,64]{1,0:T(8,128)(2,1)S(1)}, bf16[320,64]{1,0:T(8,128)(2,1)}, u32[]{:S(2)}) copy-start(bf16[320,64]{1,0:T(8,128)(2,1)} %copy.72) | copy-start | bytes 122884
  362.1 41.1 %copy-start.7 = (bf16[320,128]{1,0:T(8,128)(2,1)}, bf16[320,128]{1,0:T(8,128)(2,1)S(1)}, u32[]{:S(2)}) copy-start(bf16[320,128]{1,0:T(8,128)(2,1)S(1)} %get-tuple-element.6) | copy-start | bytes 245764
  401.6 3.1 copy-start.2
  407.6 16.3 %copy-start.1 = (bf16[2560,640]{1,0:T(8,128)(2,1)S(1)}, bf16[2560,640]{1,0:T(8,128)(2,1)}, u32[]{:S(2)}) copy-start(bf16[2560,640]{1,0:T(8,128)(2,1)} %param.25) | copy-start | bytes 9830404
Sparse Core Ops, SparseCore 0:
  17.8 19.8 all-gather.6
  66.0 213.3 all-gather.4
  281.7 6.3 reduce-scatter.6
  295.0 63.1 reduce-scatter.4
  363.0 38.6 all-gather.8

commit v2 on v1

--- a/solution.py
+++ b/solution.py
@@ -1,6 +1,10 @@
+import functools
+
 import jax
 import jax.numpy as jnp
 from jax import lax
+from jax.experimental import pallas as pl
+from jax.experimental.pallas import tpu as pltpu
 from jax.sharding import PartitionSpec as P
 
 HEAD_DIM = 128
@@ -101,6 +105,300 @@
     product = gram(first[0], second[0], first[1], second[1]) + gram(third[0], fourth[0], third[1], fourth[1])
     scores = jnp.sum(product.reshape(n_cand, seq, -1, seq), axis=(1, 3))
     return lax.all_gather(scores, "mp", axis=0, tiled=True)
+
+
+def remote(src, dst, send_sem, recv_sem, device_id):
+    return pltpu.make_async_remote_copy(
+        src_ref=src, dst_ref=dst, send_sem=send_sem, recv_sem=recv_sem,
+        device_id=device_id, device_id_type=pl.DeviceIdType.MESH,
+    )
+
+
+def kernel(
+    n_dp,
+    cand_len, val_len, cand_x, val_x, cand_grad, val_grad, cand_attn, val_attn, cand_probs, val_probs,
+    out_weight, input_proj, grad_proj, attn_proj, value_proj,
+    scores,
+    g_own, x_own, attn, c_probs, v_probs, weight, g_all, x_half, x_other, x_all, fold, mixed,
+    att_send, att_recv, b_own, b_send, b_recv, factor_own, factor_sib, factor_val, out_own, out_sib,
+    load_sem, g_send, g_recv, x_send, x_recv, hop_send, fold_send, fold_recv, bs_send, bs_recv,
+    f_send, f_recv, pair_send, pair_recv,
+):
+    dp, mp = lax.axis_index("dp"), lax.axis_index("mp")
+    sibling = {"mp": 1 - mp}
+    seq = c_probs.shape[2]
+    n_cand, n_val = c_probs.shape[0] // 2, v_probs.shape[0] // 2
+    count = n_cand + n_val
+    rows_c, rows_v = n_cand * seq, n_val * seq
+    tokens = rows_c + rows_v
+    features = weight.shape[1]
+    local_heads = c_probs.shape[1]
+    local_kv = value_proj.shape[0] // HEAD_DIM
+    group = local_heads // local_kv
+    kb = value_proj.shape[1]
+    ka = input_proj.shape[1]
+
+    barrier = pltpu.get_barrier_semaphore()
+    for step in range(1, n_dp):
+        pl.semaphore_signal(barrier, inc=1, device_id={"dp": lax.rem(dp + step, n_dp)}, device_id_type=pl.DeviceIdType.MESH)
+    pl.semaphore_signal(barrier, inc=1, device_id=sibling, device_id_type=pl.DeviceIdType.MESH)
+
+    own_c = pl.ds(pl.multiple_of(mp * rows_c, 16), rows_c)
+    own_v = pl.ds(pl.multiple_of(mp * rows_v, 16), rows_v)
+    mine = pl.ds(pl.multiple_of(dp * features, 128), features)
+    all_c = cand_attn.shape[0]
+    loads = []
+    pairs = (
+        (cand_probs, c_probs), (val_probs, v_probs), (out_weight, weight),
+        (cand_grad.at[own_c], g_own.at[pl.ds(0, rows_c)]), (val_grad.at[own_v], g_own.at[pl.ds(rows_c, rows_v)]),
+        (cand_attn, attn.at[pl.ds(0, all_c)]), (val_attn, attn.at[pl.ds(all_c, val_attn.shape[0])]),
+        (cand_x.at[own_c], x_own.at[pl.ds(0, rows_c)]), (val_x.at[own_v], x_own.at[pl.ds(rows_c, rows_v)]),
+        (cand_grad.at[own_c, mine], g_all.at[dp, pl.ds(0, rows_c)]),
+        (val_grad.at[own_v, mine], g_all.at[dp, pl.ds(rows_c, rows_v)]),
+    )
+    for slot, (src, dst) in enumerate(pairs):
+        load = pltpu.make_async_copy(src, dst, load_sem.at[slot])
+        load.start()
+        loads.append(load)
+    pl.semaphore_wait(barrier, n_dp)
+
+    g_copies = []
+    for step in range(1, n_dp):
+        peer = lax.rem(dp + step, n_dp)
+        theirs = pl.ds(pl.multiple_of(peer * features, 128), features)
+        for part, (src, rows, at) in enumerate(((cand_grad, own_c, pl.ds(0, rows_c)), (val_grad, own_v, pl.ds(rows_c, rows_v)))):
+            copy = remote(src.at[rows, theirs], g_all.at[dp, at], g_send.at[part, peer], g_recv.at[part, dp], {"dp": peer})
+            copy.start()
+            g_copies.append(copy)
+
+    loads[0].wait()
+    loads[1].wait()
+    width = local_heads * seq
+    eye = (lax.broadcasted_iota(jnp.int32, (seq, seq), 0) == lax.broadcasted_iota(jnp.int32, (seq, seq), 1)).astype(jnp.bfloat16)
+    query = lax.rem(lax.broadcasted_iota(jnp.int32, (seq, width), 1), seq)
+
+    def turn(source, lengths, per_half, offset):
+        def body(e, carry):
+            flat = source[e].reshape(width, seq)
+            turned = dot(eye, flat, (1, 1))
+            turned = jnp.where(query < lengths[e], turned, 0.0).astype(jnp.bfloat16)
+            at = pl.multiple_of((offset + lax.rem(e, per_half)) * seq, 16)
+            x_half[lax.div(e, per_half), pl.ds(at, seq), :] = turned
+            return carry
+        lax.fori_loop(0, 2 * per_half, body, 0)
+
+    turn(c_probs, cand_len, n_cand, 0)
+    turn(v_probs, val_len, n_val, n_cand)
+    x_pair = remote(x_half.at[1 - mp], x_other, pair_send.at[0], pair_recv.at[0], sibling)
+    x_pair.start()
+
+    loads[2].wait()
+    fold_copies = []
+    for k in range(local_kv):
+        proj = value_proj[k * HEAD_DIM:(k + 1) * HEAD_DIM, :].T
+        for h in range(group):
+            at = (k * group + h) * HEAD_DIM
+            rows = pl.ds(pl.multiple_of((mp * local_heads + k * group + h) * kb, 128), kb)
+            fold[rows, :] = dot(proj, weight[at:at + HEAD_DIM, :], (1, 0)).astype(jnp.bfloat16)
+        span = pl.ds(pl.multiple_of((mp * local_heads + k * group) * kb, 128), group * kb)
+        copy = remote(fold.at[span], fold.at[span], fold_send.at[k], fold_recv.at[k], sibling)
+        copy.start()
+        fold_copies.append(copy)
+        if k == 0:
+            x_pair.wait()
+            first, other = x_half[mp], x_other[...]
+            low, high = jnp.where(mp == 0, first, other), jnp.where(mp == 0, other, first)
+            x_all[dp] = jnp.concatenate([low, high], axis=1)
+            partner = {"dp": dp + 1 - 2 * lax.rem(dp, 2)}
+            x_copies = []
+            for step in range(2, n_dp, 2):
+                peer = lax.rem(dp + step, n_dp)
+                copy = remote(x_all.at[dp], x_all.at[dp], x_send.at[peer], x_recv.at[dp], {"dp": peer})
+                copy.start()
+                x_copies.append(copy)
+            copy = remote(x_all.at[dp], x_all.at[dp], hop_send.at[dp], x_recv.at[dp], partner)
+            copy.start()
+            x_copies.append(copy)
+
+    loads[5].wait()
+    loads[6].wait()
+    for half in range(2):
+        att_send[half, pl.ds(0, rows_c), :] = dot(attn[half * rows_c:(half + 1) * rows_c, :], attn_proj[...], (1, 0))
+        att_send[half, pl.ds(rows_c, rows_v), :] = dot(
+            attn[all_c + half * rows_v:all_c + (half + 1) * rows_v, :], attn_proj[...], (1, 0))
+    att_pair = remote(att_send.at[1 - mp], att_recv, pair_send.at[1], pair_recv.at[1], sibling)
+    att_pair.start()
+    for slot in (3, 4, 7, 8, 9, 10):
+        loads[slot].wait()
+    a_in = dot(x_own[...], input_proj[...], (1, 0)).astype(jnp.bfloat16)
+    b_own[...] = dot(g_own[...], grad_proj[...], (1, 0))
+    position = lax.broadcasted_iota(jnp.int32, (seq, kb), 0)
+    for e in range(count):
+        live = cand_len[mp * n_cand + e] if e < n_cand else val_len[mp * n_val + e - n_cand]
+        at = slice(e * seq, (e + 1) * seq)
+        b_own[at, :] = jnp.where(position < live, b_own[at, :], 0.0)
+    att_pair.wait()
+    a_att = (att_send[mp] + att_recv[...]).astype(jnp.bfloat16)
+    factor_own[:, 0:2 * ka] = jnp.concatenate([a_att, a_in], axis=1)
+
+    for step in range(2, n_dp, 2):
+        source = lax.rem(dp - step + n_dp, n_dp)
+        remote(x_all.at[source], x_all.at[source], x_send.at[source], x_recv.at[source], partner).wait_recv()
+        copy = remote(x_all.at[source], x_all.at[source], hop_send.at[source], x_recv.at[source], partner)
+        copy.start()
+        x_copies.append(copy)
+    for k in range(local_kv):
+        span = pl.ds(pl.multiple_of(((1 - mp) * local_heads + k * group) * kb, 128), group * kb)
+        remote(fold.at[span], fold.at[span], fold_send.at[k], fold_recv.at[k], sibling).wait_recv()
+
+    heads = 2 * local_heads
+    batch = 4
+
+    def block(source):
+        def heads_step(c, carry):
+            rows = pl.ds(pl.multiple_of(c * batch * kb, 128), batch * kb)
+            part = dot(g_all[source], fold[rows, :], (1, 1)).astype(jnp.bfloat16)
+            for h in range(batch):
+                at = pl.ds(pl.multiple_of((c * batch + h) * seq, 16), seq)
+                mixed[:, at, :] = part[:, h * kb:(h + 1) * kb].reshape(count, seq, kb)
+            return carry
+        lax.fori_loop(0, heads // batch, heads_step, 0)
+
+        def prompt_step(e, carry):
+            at = pl.ds(pl.multiple_of(e * seq, 16), seq)
+            b_send[source, at, :] = dot(x_all[source, at, :], mixed[e], (1, 0)).astype(jnp.bfloat16)
+            return carry
+        lax.fori_loop(0, count, prompt_step, 0, unroll=4)
+
+    block(dp)
+    b_val = b_send[dp].astype(jnp.float32)
+
+    order = range(1, n_dp)
+
+    def receive(step, waited):
+        source = lax.rem(dp - step + n_dp, n_dp)
+        for part, at in enumerate((pl.ds(0, rows_c), pl.ds(rows_c, rows_v))):
+            remote(g_all.at[source, at], g_all.at[source, at], g_send.at[part, source], g_recv.at[part, source], {"dp": source}).wait_recv()
+        if not waited:
+            remote(x_all.at[source], x_all.at[source], hop_send.at[source], x_recv.at[source], {"dp": source}).wait_recv()
+        block(source)
+        copy = remote(b_send.at[source], b_recv.at[dp], bs_send.at[source], bs_recv.at[dp], {"dp": source})
+        copy.start()
+        return copy
+
+    b_copies = [receive(step, step % 2 == 0) for step in order]
+    for step in order:
+        source = lax.rem(dp - step + n_dp, n_dp)
+        remote(b_recv.at[source], b_recv.at[source], bs_send.at[source], bs_recv.at[source], {"dp": source}).wait_recv()
+        b_val = b_val + b_recv[source].astype(jnp.float32)
+
+    low_out, low_val = b_own[...].astype(jnp.bfloat16), b_val.astype(jnp.bfloat16)
+    square = gram(a_att, low_out, a_att, low_out) + gram(a_in, low_val, a_in, low_val)
+    one = lax.div(lax.broadcasted_iota(jnp.int32, (tokens, tokens), 0), seq)
+    two = lax.div(lax.broadcasted_iota(jnp.int32, (tokens, tokens), 1), seq)
+    same = one == two
+    square = jnp.sum(jnp.where(same, square, 0.0), axis=1, keepdims=True)
+    square = jnp.broadcast_to(square, (tokens, 128))
+    total = lax.dot_general(same.astype(jnp.float32), square, (((1,), (0,)), ((), ())),
+                            precision=lax.Precision.HIGHEST, preferred_element_type=jnp.float32)
+    scale = lax.rsqrt(jnp.maximum(total[:, 0:1], 0.0) + EPS)
+    factor_own[:, 2 * ka:2 * ka + kb] = (b_own[...] * scale).astype(jnp.bfloat16)
+    factor_own[:, 2 * ka + kb:] = (b_val * scale).astype(jnp.bfloat16)
+    f_copies = []
+    val_rows, cand_rows = pl.ds(rows_c, rows_v), pl.ds(0, rows_c)
+    for step in order:
+        peer = lax.rem(dp + step, n_dp)
+        copy = remote(factor_own.at[val_rows], factor_val.at[dp], f_send.at[peer], f_recv.at[dp], {"dp": peer})
+        copy.start()
+        f_copies.append(copy)
+    f_pair = remote(factor_own.at[cand_rows], factor_sib, pair_send.at[2], pair_recv.at[2], sibling)
+    f_pair.start()
+    for copy in g_copies + x_copies + fold_copies + b_copies:
+        copy.wait_send()
+    f_pair.wait()
+
+    first, other = factor_own[0:rows_c, :], factor_sib[...]
+    cand = jnp.concatenate([jnp.where(mp == 0, first, other), jnp.where(mp == 0, other, first)], axis=0)
+
+    def compare(val, source):
+        product = gram(cand[:, 0:ka], cand[:, 2 * ka:2 * ka + kb], val[:, 0:ka], val[:, 2 * ka:2 * ka + kb])
+        product += gram(cand[:, ka:2 * ka], cand[:, 2 * ka + kb:], val[:, ka:2 * ka], val[:, 2 * ka + kb:])
+        product = jnp.sum(product.reshape(2 * n_cand, seq, rows_v), axis=1)
+        row = lax.broadcasted_iota(jnp.int32, (rows_v, out_own.shape[1]), 0)
+        column = lax.broadcasted_iota(jnp.int32, (rows_v, out_own.shape[1]), 1)
+        place = column == (2 * source + mp) * n_val + lax.div(row, seq)
+        return lax.dot_general(product, place.astype(jnp.float32), (((1,), (0,)), ((), ())),
+                               precision=lax.Precision.HIGHEST, preferred_element_type=jnp.float32)
+
+    result = compare(factor_own[rows_c:, :], dp)
+    for step in order:
+        source = lax.rem(dp - step + n_dp, n_dp)
+        remote(factor_val.at[source], factor_val.at[source], f_send.at[source], f_recv.at[source], {"dp": source}).wait_recv()
+        result += compare(factor_val[source], source)
+    out_own[...] = result
+    out_pair = remote(out_own, out_sib, pair_send.at[3], pair_recv.at[3], sibling)
+    out_pair.start()
+    for copy in f_copies:
+        copy.wait_send()
+    out_pair.wait()
+    scores[...] = out_own[...] + out_sib[...]
+
+
+def fused(n_dp, cand_x, val_x, cand_grad, val_grad, cand_attn, val_attn, cand_probs, val_probs,
+          cand_len, val_len, out_weight, input_proj, grad_proj, attn_proj, value_proj):
+    seq, width = cand_x.shape[1:]
+    n_cand, n_val = cand_x.shape[0] // 2, val_x.shape[0] // 2
+    tokens = (n_cand + n_val) * seq
+    rows_c, rows_v = n_cand * seq, n_val * seq
+    features = out_weight.shape[1]
+    heads = cand_probs.shape[1]
+    ka, kb = input_proj.shape[1], grad_proj.shape[1]
+    local_kv = value_proj.shape[0] // HEAD_DIM
+    bf16, f32 = jnp.bfloat16, jnp.float32
+    flat = [part.reshape(-1, part.shape[2]) for part in (cand_x, val_x, cand_grad, val_grad, cand_attn, val_attn)]
+    out = jax.ShapeDtypeStruct((2 * n_cand, n_val * 2 * n_dp), f32)
+    smem, vmem, hbm = (pl.BlockSpec(memory_space=space) for space in (pltpu.SMEM, pltpu.VMEM, pl.ANY))
+    dma = pltpu.SemaphoreType.DMA
+    factor = 2 * ka + 2 * kb
+    return pl.pallas_call(
+        functools.partial(kernel, n_dp),
+        out_shape=out,
+        in_specs=[smem] * 2 + [hbm] * 9 + [vmem] * 4,
+        out_specs=vmem,
+        scratch_shapes=[
+            pltpu.VMEM((tokens, width), bf16),
+            pltpu.VMEM((tokens, width), bf16),
+            pltpu.VMEM((2 * tokens, flat[4].shape[1]), bf16),
+            pltpu.VMEM(cand_probs.shape, bf16),
+            pltpu.VMEM(val_probs.shape, bf16),
+            pltpu.VMEM(out_weight.shape, bf16),
+            pltpu.VMEM((n_dp, tokens, features), bf16),
+            pltpu.VMEM((2, tokens, heads * seq), bf16),
+            pltpu.VMEM((tokens, heads * seq), bf16),
+            pltpu.VMEM((n_dp, tokens, 2 * heads * seq), bf16),
+            pltpu.VMEM((2 * heads * kb, features), bf16),
+            pltpu.VMEM((n_cand + n_val, 2 * heads * seq, kb), bf16),
+            pltpu.VMEM((2, tokens, ka), f32),
+            pltpu.VMEM((tokens, ka), f32),
+            pltpu.VMEM((tokens, kb), f32),
+            pltpu.VMEM((n_dp, tokens, kb), bf16),
+            pltpu.VMEM((n_dp, tokens, kb), bf16),
+            pltpu.VMEM((tokens, factor), bf16),
+            pltpu.VMEM((rows_c, factor), bf16),
+            pltpu.VMEM((n_dp, rows_v, factor), bf16),
+            pltpu.VMEM(out.shape, f32),
+            pltpu.VMEM(out.shape, f32),
+            dma((11,)),
+            dma((2, n_dp)), dma((2, n_dp)),
+            dma((n_dp,)), dma((n_dp,)), dma((n_dp,)),
+            dma((local_kv,)), dma((local_kv,)),
+            dma((n_dp,)), dma((n_dp,)), dma((n_dp,)), dma((n_dp,)),
+            dma((4,)), dma((4,)),
+        ],
+        compiler_params=pltpu.CompilerParams(
+            collective_id=0, has_side_effects=True, vmem_limit_bytes=60 * 1024 * 1024
+        ),
+    )(cand_len, val_len, *flat, cand_probs, val_probs, out_weight, input_proj, grad_proj, attn_proj, value_proj)
 
 
 def solution(mesh):
@@ -122,8 +420,13 @@
         P("mp", None),
     )
 
+    n_dp, n_mp = mesh.shape["dp"], mesh.shape["mp"]
+
     def body(*args):
-        return local(mesh.shape["mp"], *args)
+        features, heads = args[10].shape[1], args[6].shape[1]
+        if n_mp == 2 and n_dp % 2 == 0 and features % 128 == 0 and heads % 2 == 0:
+            return fused(n_dp, *args)
+        return local(n_mp, *args)
 
     return jax.shard_map(
         body, mesh=mesh, in_specs=placed, out_specs=P(("grp", "dp"), None), check_vma=False

time: 432 us -> 196 us (0.45)
  waiting for transfers between devices: 231 us -> 0 us
  Pallas kernels: 0 us -> 181 us
  local copies, waits for them, and re-layouts: 91.1 us -> 12 us
  matrix products: 60.6 us -> 0 us
  other arithmetic: 19.7 us -> 0 us
  between operations: 13.4 us -> 0.01 us
  starting transfers between devices: 7.77 us -> 0 us
  blocking collectives: 6.73 us -> 0 us
    pallas_call x0 -> x1, Pallas kernels: none -> 181 us  [fused(): pl.pallas_call(functools.partial(kernel, n_dp), out_shape=out, in_specs=[...]
    all_to_all x1 -> x0, waiting for transfers between devices: 125 us -> none  [local(): lax.all_to_all(grads.reshape(tokens, n_dp, features), 'dp', 1, 0, tiled=T...]
    dot_general x13 -> x0, matrix products: 58.8 us -> none  [the longest x11 39.7 us: dot(): lax.dot_general(left, right, ((contract[:1], contract[1:]), ((), ())), pr...]
    reduce_scatter x2 -> x0, waiting for transfers between devices: 53.9 us -> none  [the longest x1 53.8 us: local(): lax.psum_scatter(b_val, 'dp', scatter_dimension=0, tiled=True)]
    all_gather x3 -> x0, waiting for transfers between devices: 51.9 us -> none  [the longest x1 38.8 us: local(): theirs = lax.all_gather(factors[rows:], ('dp', 'mp'), axis=0, tiled=True)]
    unnamed x30 -> x9, local copies, waits for them, and re-layouts: 39.5 us -> 12 us
    reshape x6 -> x0, local copies, waits for them, and re-layouts: 23.2 us -> none  [the longest x1 8.43 us: local(): scores = jnp.sum(product.reshape(n_cand, seq, -1, seq), axis=(1, 3))]
    all_gather x1 -> x0, local copies, waits for them, and re-layouts: 9.55 us -> none  [local(): lax.all_gather(folded(out_weight, value_proj, heads), 'mp', axis=1, tiled...]
  transfers between devices with their start and end apart: 6 -> 0, of which waited for: 4 -> 0; matrix products, arithmetic and copies ran while one was open for 31% -> 0% of each run, Pallas kernels for 0% -> 0%
where the time goes in v2:
time: 196 us; the launch traced here: 193 us
  Pallas kernels  181 us (92%)
  local copies, waits for them, and re-layouts  12 us (6%)
    pallas_call x1, Pallas kernels, fused(): pl.pallas_call(functools.partial(kernel, n_dp), out_shape=out, in_specs=[...  181 us
    unnamed x9, local copies, waits for them, and re-layouts  12 us

profile of v2, /device:TPU:0, one launch (start us, length us, event | category | flops | bytes accessed | tf_op | source)
XLA Modules:
  0.0 193.0 jit_solution(11449081592461904708)
XLA Ops:
  0.0 0.0 copy-start.1
  0.0 2.1 %copy.19.attn_proj = bf16[2560,64]{1,0:T(8,128)(2,1)} copy(bf16[2560,64]{0,1:T(8,128)(2,1)} %param.28) | data formatting | bytes 655360 | tf_op args[13]
  2.1 0.0 copy-start
  2.1 3.9 %copy.17.val_probs = bf16[16,20,16,16]{3,2,1,0:T(8,128)(2,1)} copy(bf16[16,20,16,16]{1,3,2,0:T(8,128)(2,1)} %param.22) | data formatting | bytes 327680 | tf_op args[7]
  6.0 0.0 copy-done.1
  6.0 1.4 copy.18.input_proj
  7.4 0.0 copy-done
  7.4 3.3 %copy.16.cand_probs = bf16[24,20,16,16]{3,2,1,0:T(8,128)(2,1)} copy(bf16[24,20,16,16]{0,3,2,1:T(8,128)(2,1)S(1)} %copy-done) | data formatting | bytes 491520 | tf_op args[6]
  10.7 181.0 %shard_map.145 = f32[24,128]{1,0:T(8,128)} custom-call(s32[24]{0:T(128)} %cand_len.1, s32[16]{0:T(128)} %val_len.1, bf16[384,5120]{1,0:T(8,128)(2,1)} %bitcast.6, bf16[256,5120]{1,0:T(8,128)(2,1)} %bitcast.8, bf16[384,5120]{1,0:T(8,128)(2,1)} %bitcast.7, bf16[256,5120]{1,0:T(8,128)(2,1)} %bitcast.9, bf16[384,2560]{1,0:T(8,128)(2,1)} %bitcast.10, ...), custom_call_target="tpu_custom_call" | custom-call | tf_op jit(solution)/shard_map/pallas_call | solution.py:363
  191.7 1.3 copy.21
Async XLA Ops:
  0.0 6.0 %copy-start.1 = (bf16[5120,64]{0,1:T(8,128)(2,1)S(1)}, bf16[5120,64]{0,1:T(8,128)(2,1)}, u32[]{:S(2)}) copy-start(bf16[5120,64]{0,1:T(8,128)(2,1)} %param.26) | copy-start | bytes 1966084
  2.1 5.3 %copy-start = (bf16[24,20,16,16]{0,3,2,1:T(8,128)(2,1)S(1)}, bf16[24,20,16,16]{0,3,2,1:T(8,128)(2,1)}, u32[]{:S(2)}) copy-start(bf16[24,20,16,16]{0,3,2,1:T(8,128)(2,1)} %param.21) | copy-start | bytes 737284

commit v3 on v2

--- a/solution.py
+++ b/solution.py
@@ -112,6 +112,15 @@
         src_ref=src, dst_ref=dst, send_sem=send_sem, recv_sem=recv_sem,
         device_id=device_id, device_id_type=pl.DeviceIdType.MESH,
     )
+
+
+def flipped(index, bits, size):
+    other, bit = 0, 1
+    while bit < size:
+        own_bit = lax.rem(lax.div(index, bit), 2)
+        other = other + bit * ((1 - own_bit) if bits & bit else own_bit)
+        bit *= 2
+    return other
 
 
 def kernel(
@@ -136,11 +145,11 @@
     local_kv = value_proj.shape[0] // HEAD_DIM
     group = local_heads // local_kv
     kb = value_proj.shape[1]
-    ka = input_proj.shape[1]
+    ka = input_proj.shape[0]
 
     barrier = pltpu.get_barrier_semaphore()
     for step in range(1, n_dp):
-        pl.semaphore_signal(barrier, inc=1, device_id={"dp": lax.rem(dp + step, n_dp)}, device_id_type=pl.DeviceIdType.MESH)
+        pl.semaphore_signal(barrier, inc=1, device_id={"dp": flipped(dp, step, n_dp)}, device_id_type=pl.DeviceIdType.MESH)
     pl.semaphore_signal(barrier, inc=1, device_id=sibling, device_id_type=pl.DeviceIdType.MESH)
 
     own_c = pl.ds(pl.multiple_of(mp * rows_c, 16), rows_c)
@@ -162,14 +171,59 @@
         loads.append(load)
     pl.semaphore_wait(barrier, n_dp)
 
+    near = [2, 1, 3] if n_dp > 2 else [1]
+    far = list(range(4, n_dp))
+    order = near + far
+    spread = sorted(order, key=lambda k: (near.index(k) * len(far) // len(near) + 0.5) if k in near else far.index(k))
+    early, late = spread[:4], spread[4:]
     g_copies = []
-    for step in range(1, n_dp):
-        peer = lax.rem(dp + step, n_dp)
+
+    def send_tokens(step):
+        peer = flipped(dp, step, n_dp)
         theirs = pl.ds(pl.multiple_of(peer * features, 128), features)
         for part, (src, rows, at) in enumerate(((cand_grad, own_c, pl.ds(0, rows_c)), (val_grad, own_v, pl.ds(rows_c, rows_v)))):
             copy = remote(src.at[rows, theirs], g_all.at[dp, at], g_send.at[part, peer], g_recv.at[part, dp], {"dp": peer})
             copy.start()
             g_copies.append(copy)
+
+    for step in early:
+        send_tokens(step)
+
+    line, place = n_dp // 2, lax.div(dp, 2)
+
+    def relay_copy(source, direction):
+        slot = x_send.at[source] if direction == 1 else x_send.at[n_dp + source]
+        return remote(x_all.at[source], x_all.at[source], slot, x_recv.at[source], {"dp": dp + 2 * direction})
+
+    def relay(source, direction):
+        @pl.when((place + direction >= 0) & (place + direction < line))
+        def _():
+            relay_copy(source, direction).start()
+
+    def relay_done(source, direction):
+        @pl.when((place + direction >= 0) & (place + direction < line))
+        def _():
+            relay_copy(source, direction).wait_send()
+
+    def pass_on(source):
+        return remote(x_all.at[source], x_all.at[source], hop_send.at[source], x_recv.at[source], partner)
+
+    def at_distance(distance, act):
+        for direction in (1, -1):
+            @pl.when((place - direction * distance >= 0) & (place - direction * distance < line))
+            def _():
+                act(dp - 2 * direction * distance, direction)
+
+    def take(source, direction):
+        pass_on(source).wait_recv()
+        relay(source, direction)
+        pass_on(source).start()
+
+    def taken(source, direction):
+        relay_done(source, direction)
+        pass_on(source).wait_send()
+
+    partner = {"dp": dp + 1 - 2 * lax.rem(dp, 2)}
 
     loads[0].wait()
     loads[1].wait()
@@ -209,28 +263,25 @@
             first, other = x_half[mp], x_other[...]
             low, high = jnp.where(mp == 0, first, other), jnp.where(mp == 0, other, first)
             x_all[dp] = jnp.concatenate([low, high], axis=1)
-            partner = {"dp": dp + 1 - 2 * lax.rem(dp, 2)}
-            x_copies = []
-            for step in range(2, n_dp, 2):
-                peer = lax.rem(dp + step, n_dp)
-                copy = remote(x_all.at[dp], x_all.at[dp], x_send.at[peer], x_recv.at[dp], {"dp": peer})
-                copy.start()
-                x_copies.append(copy)
             copy = remote(x_all.at[dp], x_all.at[dp], hop_send.at[dp], x_recv.at[dp], partner)
             copy.start()
-            x_copies.append(copy)
+            x_copies = [copy]
+            for direction in (1, -1):
+                relay(dp, direction)
+            for step in late:
+                send_tokens(step)
 
     loads[5].wait()
     loads[6].wait()
     for half in range(2):
-        att_send[half, pl.ds(0, rows_c), :] = dot(attn[half * rows_c:(half + 1) * rows_c, :], attn_proj[...], (1, 0))
+        att_send[half, pl.ds(0, rows_c), :] = dot(attn[half * rows_c:(half + 1) * rows_c, :], attn_proj[...], (1, 1))
         att_send[half, pl.ds(rows_c, rows_v), :] = dot(
-            attn[all_c + half * rows_v:all_c + (half + 1) * rows_v, :], attn_proj[...], (1, 0))
+            attn[all_c + half * rows_v:all_c + (half + 1) * rows_v, :], attn_proj[...], (1, 1))
     att_pair = remote(att_send.at[1 - mp], att_recv, pair_send.at[1], pair_recv.at[1], sibling)
     att_pair.start()
     for slot in (3, 4, 7, 8, 9, 10):
         loads[slot].wait()
-    a_in = dot(x_own[...], input_proj[...], (1, 0)).astype(jnp.bfloat16)
+    a_in = dot(x_own[...], input_proj[...], (1, 1)).astype(jnp.bfloat16)
     b_own[...] = dot(g_own[...], grad_proj[...], (1, 0))
     position = lax.broadcasted_iota(jnp.int32, (seq, kb), 0)
     for e in range(count):
@@ -241,12 +292,8 @@
     a_att = (att_send[mp] + att_recv[...]).astype(jnp.bfloat16)
     factor_own[:, 0:2 * ka] = jnp.concatenate([a_att, a_in], axis=1)
 
-    for step in range(2, n_dp, 2):
-        source = lax.rem(dp - step + n_dp, n_dp)
-        remote(x_all.at[source], x_all.at[source], x_send.at[source], x_recv.at[source], partner).wait_recv()
-        copy = remote(x_all.at[source], x_all.at[source], hop_send.at[source], x_recv.at[source], partner)
-        copy.start()
-        x_copies.append(copy)
+    if line > 1:
+        at_distance(1, take)
     for k in range(local_kv):
         span = pl.ds(pl.multiple_of(((1 - mp) * local_heads + k * group) * kb, 128), group * kb)
         remote(fold.at[span], fold.at[span], fold_send.at[k], fold_recv.at[k], sibling).wait_recv()
@@ -273,10 +320,8 @@
     block(dp)
     b_val = b_send[dp].astype(jnp.float32)
 
-    order = range(1, n_dp)
-
     def receive(step, waited):
-        source = lax.rem(dp - step + n_dp, n_dp)
+        source = flipped(dp, step, n_dp)
         for part, at in enumerate((pl.ds(0, rows_c), pl.ds(rows_c, rows_v))):
             remote(g_all.at[source, at], g_all.at[source, at], g_send.at[part, source], g_recv.at[part, source], {"dp": source}).wait_recv()
         if not waited:
@@ -286,9 +331,18 @@
         copy.start()
         return copy
 
-    b_copies = [receive(step, step % 2 == 0) for step in order]
+    b_copies, hops = [], 2
+    for turn_index, step in enumerate(order):
+        if turn_index in (1, 3) and hops < line:
+            at_distance(hops, take)
+            hops += 1
+        if step >= 4:
+            while hops < line:
+                at_distance(hops, take)
+                hops += 1
+        b_copies.append(receive(step, step % 2 == 0))
     for step in order:
-        source = lax.rem(dp - step + n_dp, n_dp)
+        source = flipped(dp, step, n_dp)
         remote(b_recv.at[source], b_recv.at[source], bs_send.at[source], bs_recv.at[source], {"dp": source}).wait_recv()
         b_val = b_val + b_recv[source].astype(jnp.float32)
 
@@ -307,12 +361,16 @@
     f_copies = []
     val_rows, cand_rows = pl.ds(rows_c, rows_v), pl.ds(0, rows_c)
     for step in order:
-        peer = lax.rem(dp + step, n_dp)
+        peer = flipped(dp, step, n_dp)
         copy = remote(factor_own.at[val_rows], factor_val.at[dp], f_send.at[peer], f_recv.at[dp], {"dp": peer})
         copy.start()
         f_copies.append(copy)
     f_pair = remote(factor_own.at[cand_rows], factor_sib, pair_send.at[2], pair_recv.at[2], sibling)
     f_pair.start()
+    for direction in (1, -1):
+        relay_done(dp, direction)
+    for distance in range(1, line):
+        at_distance(distance, taken)
     for copy in g_copies + x_copies + fold_copies + b_copies:
         copy.wait_send()
     f_pair.wait()
@@ -332,7 +390,7 @@
 
     result = compare(factor_own[rows_c:, :], dp)
     for step in order:
-        source = lax.rem(dp - step + n_dp, n_dp)
+        source = flipped(dp, step, n_dp)
         remote(factor_val.at[source], factor_val.at[source], f_send.at[source], f_recv.at[source], {"dp": source}).wait_recv()
         result += compare(factor_val[source], source)
     out_own[...] = result
@@ -390,7 +448,7 @@
             pltpu.VMEM(out.shape, f32),
             dma((11,)),
             dma((2, n_dp)), dma((2, n_dp)),
-            dma((n_dp,)), dma((n_dp,)), dma((n_dp,)),
+            dma((2 * n_dp,)), dma((n_dp,)), dma((n_dp,)),
             dma((local_kv,)), dma((local_kv,)),
             dma((n_dp,)), dma((n_dp,)), dma((n_dp,)), dma((n_dp,)),
             dma((4,)), dma((4,)),
@@ -398,7 +456,7 @@
         compiler_params=pltpu.CompilerParams(
             collective_id=0, has_side_effects=True, vmem_limit_bytes=60 * 1024 * 1024
         ),
-    )(cand_len, val_len, *flat, cand_probs, val_probs, out_weight, input_proj, grad_proj, attn_proj, value_proj)
+    )(cand_len, val_len, *flat, cand_probs, val_probs, out_weight, input_proj.T, grad_proj, attn_proj.T, value_proj)
 
 
 def solution(mesh):
@@ -424,7 +482,7 @@
 
     def body(*args):
         features, heads = args[10].shape[1], args[6].shape[1]
-        if n_mp == 2 and n_dp % 2 == 0 and features % 128 == 0 and heads % 2 == 0:
+        if n_mp == 2 and n_dp in (4, 8, 16) and features % 128 == 0 and heads % 2 == 0:
             return fused(n_dp, *args)
         return local(n_mp, *args)
 

time: 196 us -> 167 us (0.85)
  Pallas kernels: 181 us -> 157 us
  local copies, waits for them, and re-layouts: 12 us -> 8.48 us
    pallas_call x1, Pallas kernels: 181 us -> 157 us  [fused(): pl.pallas_call(functools.partial(kernel, n_dp), out_shape=out, in_specs=[...]
    unnamed x9 -> x5, local copies, waits for them, and re-layouts: 12 us -> 8.48 us
where the time goes in v3:
time: 167 us; the launch traced here: 166 us
  Pallas kernels  157 us (94%)
  local copies, waits for them, and re-layouts  8.48 us (5%)
    pallas_call x1, Pallas kernels, fused(): pl.pallas_call(functools.partial(kernel, n_dp), out_shape=out, in_specs=[...  157 us
    unnamed x5, local copies, waits for them, and re-layouts  8.48 us

profile of v3, /device:TPU:0, one launch (start us, length us, event | category | flops | bytes accessed | tf_op | source)
XLA Modules:
  0.0 165.7 jit_solution(10892905367117397771)
XLA Ops:
  0.0 0.0 copy-start
  0.0 3.9 %copy.17.val_probs = bf16[16,20,16,16]{3,2,1,0:T(8,128)(2,1)} copy(bf16[16,20,16,16]{1,3,2,0:T(8,128)(2,1)} %param.22) | data formatting | bytes 327680 | tf_op args[7]
  3.9 0.0 copy-done
  3.9 3.3 %copy.16.cand_probs = bf16[24,20,16,16]{3,2,1,0:T(8,128)(2,1)} copy(bf16[24,20,16,16]{0,3,2,1:T(8,128)(2,1)S(1)} %copy-done) | data formatting | bytes 491520 | tf_op args[6]
  7.2 157.3 %shard_map.145 = f32[24,128]{1,0:T(8,128)} custom-call(s32[24]{0:T(128)} %cand_len.1, s32[16]{0:T(128)} %val_len.1, bf16[384,5120]{1,0:T(8,128)(2,1)} %bitcast.8, bf16[256,5120]{1,0:T(8,128)(2,1)} %bitcast.10, bf16[384,5120]{1,0:T(8,128)(2,1)} %bitcast.9, bf16[256,5120]{1,0:T(8,128)(2,1)} %bitcast.11, bf16[384,2560]{1,0:T(8,128)(2,1)} %bitcast.12, ...), custom_call_target="tpu_custom_call" | custom-call | tf_op jit(solution)/shard_map/pallas_call | solution.py:421
  164.4 1.3 copy.19
Async XLA Ops:
  0.0 3.9 %copy-start = (bf16[24,20,16,16]{0,3,2,1:T(8,128)(2,1)S(1)}, bf16[24,20,16,16]{0,3,2,1:T(8,128)(2,1)}, u32[]{:S(2)}) copy-start(bf16[24,20,16,16]{0,3,2,1:T(8,128)(2,1)} %param.21) | copy-start | bytes 737284

commit v4 on v3

--- a/solution.py
+++ b/solution.py
@@ -131,7 +131,7 @@
     g_own, x_own, attn, c_probs, v_probs, weight, g_all, x_half, x_other, x_all, fold, mixed,
     att_send, att_recv, b_own, b_send, b_recv, factor_own, factor_sib, factor_val, out_own, out_sib,
     load_sem, g_send, g_recv, x_send, x_recv, hop_send, fold_send, fold_recv, bs_send, bs_recv,
-    f_send, f_recv, pair_send, pair_recv,
+    f_send, f_recv, f_hop, pair_send, pair_recv,
 ):
     dp, mp = lax.axis_index("dp"), lax.axis_index("mp")
     sibling = {"mp": 1 - mp}
@@ -359,43 +359,52 @@
     factor_own[:, 2 * ka:2 * ka + kb] = (b_own[...] * scale).astype(jnp.bfloat16)
     factor_own[:, 2 * ka + kb:] = (b_val * scale).astype(jnp.bfloat16)
     f_copies = []
-    val_rows, cand_rows = pl.ds(rows_c, rows_v), pl.ds(0, rows_c)
-    for step in order:
-        peer = flipped(dp, step, n_dp)
-        copy = remote(factor_own.at[val_rows], factor_val.at[dp], f_send.at[peer], f_recv.at[dp], {"dp": peer})
+    cand_rows = pl.ds(0, rows_c)
+    factor_val[dp] = factor_own[rows_c:, :]
+
+    def send_factor(source, slot, target):
+        copy = remote(factor_val.at[source], factor_val.at[source], slot, f_recv.at[source], target)
         copy.start()
         f_copies.append(copy)
+
+    for step in [k for k in far + near if k % 2 == 0]:
+        peer = flipped(dp, step, n_dp)
+        send_factor(dp, f_send.at[peer], {"dp": peer})
+    send_factor(dp, f_hop.at[dp], partner)
     f_pair = remote(factor_own.at[cand_rows], factor_sib, pair_send.at[2], pair_recv.at[2], sibling)
     f_pair.start()
+    def factor_arrives(step):
+        source = flipped(dp, step, n_dp)
+        remote(factor_val.at[source], factor_val.at[source], f_send.at[source], f_recv.at[source], partner).wait_recv()
+        return source
+
+    for step in [k for k in near + far if k % 2 == 0]:
+        source = factor_arrives(step)
+        send_factor(source, f_hop.at[source], partner)
+    f_pair.wait()
+
+    first, other = factor_own[0:rows_c, :], factor_sib[...]
+    cand = jnp.concatenate([jnp.where(mp == 0, first, other), jnp.where(mp == 0, other, first)], axis=0)
+
+    for step in [k for k in near + far if k % 2 == 1]:
+        factor_arrives(step)
+    val = factor_val[...].reshape(n_dp * rows_v, factor_val.shape[2])
+    product = gram(cand[:, 0:ka], cand[:, 2 * ka:2 * ka + kb], val[:, 0:ka], val[:, 2 * ka:2 * ka + kb])
+    product += gram(cand[:, ka:2 * ka], cand[:, 2 * ka + kb:], val[:, ka:2 * ka], val[:, 2 * ka + kb:])
+    product = jnp.sum(product.reshape(2 * n_cand, seq, n_dp * rows_v), axis=1)
+    prompt = lax.div(lax.broadcasted_iota(jnp.int32, (n_dp * rows_v, out_own.shape[1]), 0), seq)
+    column = lax.broadcasted_iota(jnp.int32, (n_dp * rows_v, out_own.shape[1]), 1)
+    chosen = column == (2 * lax.div(prompt, n_val) + mp) * n_val + lax.rem(prompt, n_val)
+    out_own[...] = lax.dot_general(product, chosen.astype(jnp.float32), (((1,), (0,)), ((), ())),
+                                   precision=lax.Precision.HIGHEST, preferred_element_type=jnp.float32)
+    out_pair = remote(out_own, out_sib, pair_send.at[3], pair_recv.at[3], sibling)
+    out_pair.start()
     for direction in (1, -1):
         relay_done(dp, direction)
     for distance in range(1, line):
         at_distance(distance, taken)
     for copy in g_copies + x_copies + fold_copies + b_copies:
         copy.wait_send()
-    f_pair.wait()
-
-    first, other = factor_own[0:rows_c, :], factor_sib[...]
-    cand = jnp.concatenate([jnp.where(mp == 0, first, other), jnp.where(mp == 0, other, first)], axis=0)
-
-    def compare(val, source):
-        product = gram(cand[:, 0:ka], cand[:, 2 * ka:2 * ka + kb], val[:, 0:ka], val[:, 2 * ka:2 * ka + kb])
-        product += gram(cand[:, ka:2 * ka], cand[:, 2 * ka + kb:], val[:, ka:2 * ka], val[:, 2 * ka + kb:])
-        product = jnp.sum(product.reshape(2 * n_cand, seq, rows_v), axis=1)
-        row = lax.broadcasted_iota(jnp.int32, (rows_v, out_own.shape[1]), 0)
-        column = lax.broadcasted_iota(jnp.int32, (rows_v, out_own.shape[1]), 1)
-        place = column == (2 * source + mp) * n_val + lax.div(row, seq)
-        return lax.dot_general(product, place.astype(jnp.float32), (((1,), (0,)), ((), ())),
-                               precision=lax.Precision.HIGHEST, preferred_element_type=jnp.float32)
-
-    result = compare(factor_own[rows_c:, :], dp)
-    for step in order:
-        source = flipped(dp, step, n_dp)
-        remote(factor_val.at[source], factor_val.at[source], f_send.at[source], f_recv.at[source], {"dp": source}).wait_recv()
-        result += compare(factor_val[source], source)
-    out_own[...] = result
-    out_pair = remote(out_own, out_sib, pair_send.at[3], pair_recv.at[3], sibling)
-    out_pair.start()
     for copy in f_copies:
         copy.wait_send()
     out_pair.wait()
@@ -450,7 +459,7 @@
             dma((2, n_dp)), dma((2, n_dp)),
             dma((2 * n_dp,)), dma((n_dp,)), dma((n_dp,)),
             dma((local_kv,)), dma((local_kv,)),
-            dma((n_dp,)), dma((n_dp,)), dma((n_dp,)), dma((n_dp,)),
+            dma((n_dp,)), dma((n_dp,)), dma((n_dp,)), dma((n_dp,)), dma((n_dp,)),
             dma((4,)), dma((4,)),
         ],
         compiler_params=pltpu.CompilerParams(

time: 167 us -> 164 us (0.982)
  Pallas kernels: 157 us -> 155 us
    pallas_call x1, Pallas kernels: 157 us -> 155 us  [fused(): pl.pallas_call(functools.partial(kernel, n_dp), out_shape=out, in_specs=[...]
where the time goes in v4:
time: 164 us
  Pallas kernels  155 us (95%)
  local copies, waits for them, and re-layouts  8.48 us (5%)
    pallas_call x1, Pallas kernels, fused(): pl.pallas_call(functools.partial(kernel, n_dp), out_shape=out, in_specs=[...  155 us
    unnamed x5, local copies, waits for them, and re-layouts  8.48 us

profile of v4, /device:TPU:0, one launch (start us, length us, event | category | flops | bytes accessed | tf_op | source)
XLA Modules:
  0.0 163.9 jit_solution(769025824769358981)
XLA Ops:
  0.0 0.0 copy-start
  0.0 3.9 %copy.17.val_probs = bf16[16,20,16,16]{3,2,1,0:T(8,128)(2,1)} copy(bf16[16,20,16,16]{1,3,2,0:T(8,128)(2,1)} %param.22) | data formatting | bytes 327680 | tf_op args[7]
  3.9 0.0 copy-done
  3.9 3.3 %copy.16.cand_probs = bf16[24,20,16,16]{3,2,1,0:T(8,128)(2,1)} copy(bf16[24,20,16,16]{0,3,2,1:T(8,128)(2,1)S(1)} %copy-done) | data formatting | bytes 491520 | tf_op args[6]
  7.2 155.4 %shard_map.145 = f32[24,128]{1,0:T(8,128)} custom-call(s32[24]{0:T(128)} %cand_len.1, s32[16]{0:T(128)} %val_len.1, bf16[384,5120]{1,0:T(8,128)(2,1)} %bitcast.8, bf16[256,5120]{1,0:T(8,128)(2,1)} %bitcast.10, bf16[384,5120]{1,0:T(8,128)(2,1)} %bitcast.9, bf16[256,5120]{1,0:T(8,128)(2,1)} %bitcast.11, bf16[384,2560]{1,0:T(8,128)(2,1)} %bitcast.12, ...), custom_call_target="tpu_custom_call" | custom-call | tf_op jit(solution)/shard_map/pallas_call | solution.py:430
  162.6 1.3 copy.19
Async XLA Ops:
  0.0 3.9 %copy-start = (bf16[24,20,16,16]{0,3,2,1:T(8,128)(2,1)S(1)}, bf16[24,20,16,16]{0,3,2,1:T(8,128)(2,1)}, u32[]{:S(2)}) copy-start(bf16[24,20,16,16]{0,3,2,1:T(8,128)(2,1)} %param.21) | copy-start | bytes 737284
